TPU v7x, 32 devices: a whole 2x2x4 slice. The times are simulated.
32 devices in a mesh: grp: 2 (over y), tile: 8 (over z, x), tm: 2 (over core).
Axes of the slice: x: 2, y: 2, z: 4, core: 2. Of those that a mesh axis runs over, the one named last changes fastest.
Arguments:
- video: bfloat16 [8, 16, 256, 128], P(('grp', 'tm'), 'tile'), parts along dimension 0, may hold values from -60 to 60
- conv_first: bfloat16 [3, 3, 3, 128, 128], replicated, may hold values from -0.109375 to 0.109375
- conv_second: bfloat16 [3, 3, 3, 128, 128], replicated, may hold values from -0.109375 to 0.109375
- gain_first: float32 [128], replicated, may hold values from 0.1 to 1.9
- shift_first: float32 [128], replicated, may hold values from -3 to 3
- gain_second: float32 [128], replicated, may hold values from 0.1 to 1.9
- shift_second: float32 [128], replicated, may hold values from -3 to 3
- bias_second: float32 [128], replicated, may hold values from -3 to 3
Outputs:
- encoded: bfloat16 [8, 16, 256, 128], P(('grp', 'tm'), 'tile'), parts along dimension 0
There are 2 independent parts, one for each index of `grp`. A program takes and returns all parts, laid end to end along the dimension named above; an argument that names none is the same for every part. Nothing has to cross between parts.
All inputs are finite; a program needn't handle non-finite values.
Results may differ from a plain program's by a relative error of at most 0.002.
Values may be sent and summed in bfloat16 or wider, within the bound.
A program may use at most 64 MiB of HBM per device.

v0:
```python
import jax
import jax.numpy as jnp
from jax import lax
from jax.sharding import PartitionSpec as P

G = 32
EPSILON = 1e-06


def passed_along(x, axis, by):
    devices = lax.axis_size(axis)
    pairs = [(i, i + by) for i in range(devices) if 0 <= i + by < devices]
    return lax.ppermute(x, axis, pairs)


def extended_2(cells, sides, width):
    for axis, dim in sides:
        count = lax.axis_size(axis)
        ends = count - 1
        head = lax.slice_in_dim(cells, 0, width, axis=dim)
        tail = lax.slice_in_dim(cells, cells.shape[dim] - width, cells.shape[dim], axis=dim)
        cells = jnp.concatenate(
            [
                lax.ppermute(tail, axis, [(i, (i + 1) % count) for i in range(ends)]),
                cells,
                lax.ppermute(head, axis, [((i + 1) % count, i) for i in range(ends)]),
            ],
            axis=dim,
        )
    return cells


def norm_stats(values, cells_group):
    channels = values.shape[-1]
    flat = values.reshape(-1, channels)
    sums = jnp.sum(flat, axis=0).reshape(G, channels // G).sum(axis=1)
    squares = jnp.sum(flat * flat, axis=0).reshape(G, channels // G).sum(axis=1)
    totals, square_sums = lax.psum((sums, squares), ("tile", "tm"))
    center_mean = totals / cells_group
    spread = square_sums / cells_group - center_mean * center_mean
    return (center_mean, spread)


def normalize(values, center_mean, spread, gain, offset):
    channels = values.shape[-1]
    scale_group = lax.rsqrt(spread + EPSILON)
    mean_chan = jnp.repeat(center_mean, channels // G)
    scale_chan = jnp.repeat(scale_group, channels // G)
    normed = (values - mean_chan) * scale_chan * gain + offset
    return jax.nn.silu(normed).astype(jnp.bfloat16)


def causal_extend(block, received):
    front_frame = block[:1]
    repeated = jnp.concatenate([front_frame, front_frame], axis=0)
    history = jnp.where(lax.axis_index("tm") == 0, repeated, received)
    return jnp.concatenate([history, block], axis=0)


def conv_block(extended, weight):
    frame_count = extended.shape[0] - 2
    row_count = extended.shape[1] - 2
    col_count = extended.shape[2]
    channels = extended.shape[3]
    padded = jnp.pad(extended, ((0, 0), (0, 0), (1, 1), (0, 0)))
    accumulated = jnp.zeros((frame_count, row_count, col_count, weight.shape[-1]), jnp.float32)
    for time_tap in range(3):
        for row_tap in range(3):
            window = padded[time_tap : time_tap + frame_count, row_tap : row_tap + row_count]
            stacked = jnp.concatenate(
                [window[:, :, col_tap : col_tap + col_count] for col_tap in range(3)], axis=-1
            )
            kernel = weight[time_tap, row_tap].reshape(3 * channels, weight.shape[-1])
            accumulated = accumulated + jnp.dot(stacked, kernel, preferred_element_type=jnp.float32)
    return accumulated


def per_device(
    video, conv_first, conv_second, gain_first, shift_first, gain_second, shift_second, bias_second
):
    span_len, row_count, col_count, channels = video.shape
    cells_group = float(
        span_len
        * lax.axis_size("tm")
        * row_count
        * lax.axis_size("tile")
        * col_count
        * (channels // G)
    )
    source = video.astype(jnp.float32)
    mean_first, spread_first = norm_stats(source, cells_group)
    hidden_first = normalize(source, mean_first, spread_first, gain_first, shift_first)
    extended = causal_extend(hidden_first, passed_along(hidden_first, "tm", 1))
    first_out = conv_block(extended_2(extended, (("tile", 1),), 1), conv_first)
    mean_second, spread_second = norm_stats(first_out, cells_group)
    hidden_second = normalize(first_out, mean_second, spread_second, gain_second, shift_second)
    second_ext = causal_extend(hidden_second, passed_along(hidden_second, "tm", 1))
    branch = conv_block(extended_2(second_ext, (("tile", 1),), 1), conv_second)
    return (source + branch + bias_second).astype(jnp.bfloat16)


def solution(mesh):
    in_specs = (P(("grp", "tm"), "tile", None, None), P(), P(), P(), P(), P(), P(), P())
    out_specs = P(("grp", "tm"), "tile", None, None)
    return jax.shard_map(
        per_device, mesh=mesh, in_specs=in_specs, out_specs=out_specs, check_vma=False
    )
```

profile of v0, /device:TPU:0, one launch (start us, length us, event | category | flops | bytes accessed | tf_op | source)
XLA Modules:
  0.0 112.3 jit_solution(9301883458631496210)
XLA Ops:
  0.0 1.1 convert_reduce_fusion
  1.3 0.1 reduce_sum.73
  1.4 0.1 reduce_sum.75
  1.5 34.9 %all-reduce.3 = (f32[32]{0:T(128)S(1)}, f32[32]{0:T(128)S(1)}) all-reduce(f32[32]{0:T(128)S(1)} %reduce_sum.75, f32[32]{0:T(128)S(1)} %reduce_sum.73), channel_id=1, replica_groups=mesh['grp'=2,'tile'=8,'tm'=2] {'tile','tm'}, use_global_device_ids=true, to_apply=%region_5.0 | all-reduce | flops 64 | bytes 512 | tf_op jit(solution)/shard_map/psum | solution.py:38
  36.5 0.1 mul.59
  36.7 0.1 sub.26
  36.8 1.2 %fusion.116 = bf16[2,2,256,128]{3,2,1,0:T(8,128)(2,1)S(1)} fusion(bf16[2,2,256,128]{3,2,1,0:T(8,128)(2,1)} %param.8, f32[128]{0:T(128)} %param.12, f32[128]{0:T(128)} %param.11, f32[128]{0:T(128)S(1)} %mul.59, f32[128]{0:T(128)S(1)} %sub.26), kind=kLoop, calls=%fused_computation.151 | loop fusion | flops 1310720 | bytes 526336 | tf_op jit(solution)/shard_map/convert_element_type | solution.py:50
  38.0 1.4 %collective-permute-start = (bf16[2,2,256,128]{3,2,1,0:T(8,128)(2,1)S(1)}, bf16[2,2,256,128]{3,2,1,0:T(8,128)(2,1)S(1)}, u32[]{:S(2)}, u32[]{:S(2)}) collective-permute-start(bf16[2,2,256,128]{3,2,1,0:T(8,128)(2,1)S(1)} %fusion.116), channel_id=1, source_target_pairs={{0,1},{2,3},{4,5},{6,7},{8,9},{10,11},{12,13},{14,15},{16,17},{18,... | collective-permute-start | bytes 786440 | tf_op jit(solution)/shard_map/ppermute | solution.py:13
  39.5 1.1 collective-permute-done
  40.7 1.3 %collective-permute-start.1 = (bf16[4,1,256,128]{3,2,1,0:T(8,128)(2,1)S(1)}, bf16[4,1,256,128]{3,2,1,0:T(8,128)(2,1)S(1)}, u32[]{:S(2)}, u32[]{:S(2)}) collective-permute-start(bf16[4,1,256,128]{3,2,1,0:T(8,128)(2,1)S(1)} %get-tuple-element.85), channel_id=1, source_target_pairs={{0,2},{2,4},{4,6},{6,8},{8,10},{10,12},{12,14},{1,3},{3,5},{5,7},{... | collective-permute-start | bytes 786440 | tf_op jit(solution)/shard_map/ppermute | solution.py:24
  42.0 1.3 %collective-permute-start.2 = (bf16[4,1,256,128]{3,2,1,0:T(8,128)(2,1)S(1)}, bf16[4,1,256,128]{3,2,1,0:T(8,128)(2,1)S(1)}, u32[]{:S(2)}, u32[]{:S(2)}) collective-permute-start(bf16[4,1,256,128]{3,2,1,0:T(8,128)(2,1)S(1)} %get-tuple-element.86), channel_id=1, source_target_pairs={{2,0},{4,2},{6,4},{8,6},{10,8},{12,10},{14,12},{3,1},{5,3},{7,5},{... | collective-permute-start | bytes 786440 | tf_op jit(solution)/shard_map/ppermute | solution.py:26
  43.4 10.6 %collective-permute-done.1 = bf16[4,1,256,128]{3,2,1,0:T(8,128)(2,1)S(1)} collective-permute-done((bf16[4,1,256,128]{3,2,1,0:T(8,128)(2,1)S(1)}, bf16[4,1,256,128]{3,2,1,0:T(8,128)(2,1)S(1)}, u32[]{:S(2)}, u32[]{:S(2)}) %collective-permute-start.1) | collective-permute-done | bytes 262176 | tf_op jit(solution)/shard_map/ppermute | solution.py:24
  54.0 0.3 fusion.11
  54.3 1.0 fusion.142
  55.2 0.1 pad_maximum_fusion.2
  55.4 0.3 fusion.147
  55.7 0.4 fusion.22
  56.0 0.4 convolution_add_fusion.15
  56.4 0.4 convolution_add_fusion.14
  56.8 0.4 convolution_add_fusion.13
  57.1 0.4 convolution_add_fusion.12
  57.5 0.4 convolution_add_fusion.11
  57.9 0.4 convolution_add_fusion.10
  58.3 0.4 convolution_add_fusion.9
  58.7 0.4 fusion.140
  59.2 0.1 reduce_sum.77
  59.4 0.1 reduce_sum.79
  59.5 29.5 %all-reduce.2 = (f32[32]{0:T(128)S(1)}, f32[32]{0:T(128)S(1)}) all-reduce(f32[32]{0:T(128)S(1)} %reduce_sum.79, f32[32]{0:T(128)S(1)} %reduce_sum.77), channel_id=1, replica_groups=mesh['grp'=2,'tile'=8,'tm'=2] {'tile','tm'}, use_global_device_ids=true, to_apply=%region_11.12 | all-reduce | flops 64 | bytes 512 | tf_op jit(solution)/shard_map/psum | solution.py:38
  89.1 0.1 mul.67
  89.3 0.1 sub.30
  89.4 0.2 multiply_convert_fusion
  89.6 1.9 %collective-permute-start.3 = (bf16[2,2,256,128]{3,2,1,0:T(8,128)(2,1)S(1)}, bf16[2,2,256,128]{3,2,1,0:T(8,128)(2,1)S(1)}, u32[]{:S(2)}, u32[]{:S(2)}) collective-permute-start(bf16[2,2,256,128]{3,2,1,0:T(8,128)(2,1)S(1)} %multiply_convert_fusion), channel_id=1, source_target_pairs={{0,1},{2,3},{4,5},{6,7},{8,9},{10,11},{12,13},{14,15},{16,17},{18,... | collective-permute-start | bytes 786440 | tf_op jit(solution)/shard_map/ppermute | solution.py:13
  91.6 1.1 collective-permute-done.3
  92.8 1.3 %collective-permute-start.4 = (bf16[4,1,256,128]{3,2,1,0:T(8,128)(2,1)S(1)}, bf16[4,1,256,128]{3,2,1,0:T(8,128)(2,1)S(1)}, u32[]{:S(2)}, u32[]{:S(2)}) collective-permute-start(bf16[4,1,256,128]{3,2,1,0:T(8,128)(2,1)S(1)} %get-tuple-element.81), channel_id=1, source_target_pairs={{0,2},{2,4},{4,6},{6,8},{8,10},{10,12},{12,14},{1,3},{3,5},{5,7},{... | collective-permute-start | bytes 786440 | tf_op jit(solution)/shard_map/ppermute | solution.py:24
  94.1 1.3 %collective-permute-start.5 = (bf16[4,1,256,128]{3,2,1,0:T(8,128)(2,1)S(1)}, bf16[4,1,256,128]{3,2,1,0:T(8,128)(2,1)S(1)}, u32[]{:S(2)}, u32[]{:S(2)}) collective-permute-start(bf16[4,1,256,128]{3,2,1,0:T(8,128)(2,1)S(1)} %get-tuple-element.82), channel_id=1, source_target_pairs={{2,0},{4,2},{6,4},{8,6},{10,8},{12,10},{14,12},{3,1},{5,3},{7,5},{... | collective-permute-start | bytes 786440 | tf_op jit(solution)/shard_map/ppermute | solution.py:26
  95.5 10.6 %collective-permute-done.4 = bf16[4,1,256,128]{3,2,1,0:T(8,128)(2,1)S(1)} collective-permute-done((bf16[4,1,256,128]{3,2,1,0:T(8,128)(2,1)S(1)}, bf16[4,1,256,128]{3,2,1,0:T(8,128)(2,1)S(1)}, u32[]{:S(2)}, u32[]{:S(2)}) %collective-permute-start.4) | collective-permute-done | bytes 262176 | tf_op jit(solution)/shard_map/ppermute | solution.py:24
  106.3 0.3 select_maximum_fusion
  106.6 1.0 fusion.141
  107.7 0.4 fusion.65
  108.1 0.4 convolution_add_fusion.7
  108.4 0.4 convolution_add_fusion.6
  108.8 0.4 convolution_add_fusion.5
  109.2 0.4 convolution_add_fusion.4
  109.6 0.4 convolution_add_fusion.3
  109.9 0.4 convolution_add_fusion.2
  110.3 0.4 convolution_add_fusion.1
  110.7 0.6 copy-done
  111.3 1.1 fusion.3
  (34 shorter events, 1.4 us)
Async XLA Ops:
  38.0 5.3 %copy-start.1 = (bf16[3,3,3,128,128]{4,3,2,1,0:T(8,128)(2,1)S(1)}, bf16[3,3,3,128,128]{4,3,2,1,0:T(8,128)(2,1)}, u32[]{:S(2)}) copy-start(bf16[3,3,3,128,128]{4,3,2,1,0:T(8,128)(2,1)} %param.9) | copy-start | bytes 2654212
  38.0 2.6 %collective-permute-start = (bf16[2,2,256,128]{3,2,1,0:T(8,128)(2,1)S(1)}, bf16[2,2,256,128]{3,2,1,0:T(8,128)(2,1)S(1)}, u32[]{:S(2)}, u32[]{:S(2)}) collective-permute-start(bf16[2,2,256,128]{3,2,1,0:T(8,128)(2,1)S(1)} %fusion.116), channel_id=1, source_target_pairs={{0,1},{2,3},{4,5},{6,7},{8,9},{10,11},{12,13},{14,15},{16,17},{18,... | collective-permute-start | bytes 786440 | tf_op jit(solution)/shard_map/ppermute | solution.py:13
  40.7 13.3 %collective-permute-start.1 = (bf16[4,1,256,128]{3,2,1,0:T(8,128)(2,1)S(1)}, bf16[4,1,256,128]{3,2,1,0:T(8,128)(2,1)S(1)}, u32[]{:S(2)}, u32[]{:S(2)}) collective-permute-start(bf16[4,1,256,128]{3,2,1,0:T(8,128)(2,1)S(1)} %get-tuple-element.85), channel_id=1, source_target_pairs={{0,2},{2,4},{4,6},{6,8},{8,10},{10,12},{12,14},{1,3},{3,5},{5,7},{... | collective-permute-start | bytes 786440 | tf_op jit(solution)/shard_map/ppermute | solution.py:24
  42.0 12.0 %collective-permute-start.2 = (bf16[4,1,256,128]{3,2,1,0:T(8,128)(2,1)S(1)}, bf16[4,1,256,128]{3,2,1,0:T(8,128)(2,1)S(1)}, u32[]{:S(2)}, u32[]{:S(2)}) collective-permute-start(bf16[4,1,256,128]{3,2,1,0:T(8,128)(2,1)S(1)} %get-tuple-element.86), channel_id=1, source_target_pairs={{2,0},{4,2},{6,4},{8,6},{10,8},{12,10},{14,12},{3,1},{5,3},{7,5},{... | collective-permute-start | bytes 786440 | tf_op jit(solution)/shard_map/ppermute | solution.py:26
  58.6 30.8 %copy-start.3 = (f32[128]{0:T(128)S(1)}, f32[128]{0:T(128)}, u32[]{:S(2)}) copy-start(f32[128]{0:T(128)} %param.14) | copy-start | bytes 1540
  58.7 30.8 %copy-start.4 = (f32[128]{0:T(128)S(1)}, f32[128]{0:T(128)}, u32[]{:S(2)}) copy-start(f32[128]{0:T(128)} %param.13) | copy-start | bytes 1540
  89.6 5.8 %copy-start.2 = (bf16[3,3,3,128,128]{4,3,2,1,0:T(8,128)(2,1)S(1)}, bf16[3,3,3,128,128]{4,3,2,1,0:T(8,128)(2,1)}, u32[]{:S(2)}) copy-start(bf16[3,3,3,128,128]{4,3,2,1,0:T(8,128)(2,1)} %param.10) | copy-start | bytes 2654212
  89.6 3.1 %collective-permute-start.3 = (bf16[2,2,256,128]{3,2,1,0:T(8,128)(2,1)S(1)}, bf16[2,2,256,128]{3,2,1,0:T(8,128)(2,1)S(1)}, u32[]{:S(2)}, u32[]{:S(2)}) collective-permute-start(bf16[2,2,256,128]{3,2,1,0:T(8,128)(2,1)S(1)} %multiply_convert_fusion), channel_id=1, source_target_pairs={{0,1},{2,3},{4,5},{6,7},{8,9},{10,11},{12,13},{14,15},{16,17},{18,... | collective-permute-start | bytes 786440 | tf_op jit(solution)/shard_map/ppermute | solution.py:13
  92.8 13.3 %collective-permute-start.4 = (bf16[4,1,256,128]{3,2,1,0:T(8,128)(2,1)S(1)}, bf16[4,1,256,128]{3,2,1,0:T(8,128)(2,1)S(1)}, u32[]{:S(2)}, u32[]{:S(2)}) collective-permute-start(bf16[4,1,256,128]{3,2,1,0:T(8,128)(2,1)S(1)} %get-tuple-element.81), channel_id=1, source_target_pairs={{0,2},{2,4},{4,6},{6,8},{8,10},{10,12},{12,14},{1,3},{3,5},{5,7},{... | collective-permute-start | bytes 786440 | tf_op jit(solution)/shard_map/ppermute | solution.py:24
  94.1 12.0 %collective-permute-start.5 = (bf16[4,1,256,128]{3,2,1,0:T(8,128)(2,1)S(1)}, bf16[4,1,256,128]{3,2,1,0:T(8,128)(2,1)S(1)}, u32[]{:S(2)}, u32[]{:S(2)}) collective-permute-start(bf16[4,1,256,128]{3,2,1,0:T(8,128)(2,1)S(1)} %get-tuple-element.82), channel_id=1, source_target_pairs={{2,0},{4,2},{6,4},{8,6},{10,8},{12,10},{14,12},{3,1},{5,3},{7,5},{... | collective-permute-start | bytes 786440 | tf_op jit(solution)/shard_map/ppermute | solution.py:26
  110.3 1.0 copy-start
  110.3 0.9 copy-start.5
where the time goes:
time: 113 us; the launch traced here: 112 us
  blocking collectives  64.4 us (57%)
  waiting for transfers between devices  23.4 us (21%)
  starting transfers between devices  8.55 us (8%)
  matrix products  7.35 us (7%)
  local copies, waits for them, and re-layouts  4.33 us (4%)
  other arithmetic  3.9 us (3%)
    psum x2, blocking collectives, norm_stats(): totals, square_sums = lax.psum((sums, squares), ('tile', 'tm'))  64.4 us
    ppermute x2, waiting for transfers between devices, extended_2(): lax.ppermute(tail, axis, [(i, (i + 1) % count) for i in range(ends)])  21.2 us
    dot_general x18, matrix products, conv_block(): jnp.dot(stacked, kernel, preferred_element_type=jnp.float32)  7.35 us
    ppermute x2, starting transfers between devices, passed_along(): return lax.ppermute(x, axis, pairs)  3.35 us
    ppermute x2, starting transfers between devices, extended_2(): lax.ppermute(tail, axis, [(i, (i + 1) % count) for i in range(ends)])  2.61 us
    ppermute x2, starting transfers between devices, extended_2(): lax.ppermute(head, axis, [((i + 1) % count, i) for i in range(ends)])  2.58 us
    slice x5, local copies, waits for them, and re-layouts, conv_block(): window[:, :, col_tap:col_tap + col_count]  2.46 us
  transfers between devices with their start and end apart: 6, of which 4 were waited for; matrix products, arithmetic and copies ran while one was open for 0% of the time, Pallas kernels for 0%

commit v1 on v0

--- a/solution.py
+++ b/solution.py
@@ -35,7 +35,7 @@
     flat = values.reshape(-1, channels)
     sums = jnp.sum(flat, axis=0).reshape(G, channels // G).sum(axis=1)
     squares = jnp.sum(flat * flat, axis=0).reshape(G, channels // G).sum(axis=1)
-    totals, square_sums = lax.psum((sums, squares), ("tile", "tm"))
+    totals, square_sums = lax.psum(lax.psum((sums, squares), "tm"), "tile")
     center_mean = totals / cells_group
     spread = square_sums / cells_group - center_mean * center_mean
     return (center_mean, spread)

time: 113 us -> 95.5 us (0.85)
  blocking collectives: 64.4 us -> 47.6 us
    psum x2 -> x4, blocking collectives: 64.4 us -> 47.6 us  [norm_stats(): totals, square_sums = lax.psum(lax.psum((sums, squares), 'tm'), 'tile')]
where the time goes in v1:
time: 95.5 us; the launch traced here: 95.1 us
  blocking collectives  47.6 us (50%)
  waiting for transfers between devices  23.2 us (24%)
  starting transfers between devices  8.23 us (9%)
  matrix products  7.36 us (8%)
  local copies, waits for them, and re-layouts  4.33 us (5%)
  other arithmetic  3.9 us (4%)
    psum x4, blocking collectives, norm_stats(): totals, square_sums = lax.psum(lax.psum((sums, squares), 'tm'), 'tile')  47.6 us
    ppermute x2, waiting for transfers between devices, extended_2(): lax.ppermute(tail, axis, [(i, (i + 1) % count) for i in range(ends)])  21 us
    dot_general x18, matrix products, conv_block(): jnp.dot(stacked, kernel, preferred_element_type=jnp.float32)  7.36 us
    ppermute x2, starting transfers between devices, passed_along(): return lax.ppermute(x, axis, pairs)  2.87 us
    ppermute x2, starting transfers between devices, extended_2(): lax.ppermute(tail, axis, [(i, (i + 1) % count) for i in range(ends)])  2.77 us
    ppermute x2, starting transfers between devices, extended_2(): lax.ppermute(head, axis, [((i + 1) % count, i) for i in range(ends)])  2.58 us
    slice x5, local copies, waits for them, and re-layouts, conv_block(): window[:, :, col_tap:col_tap + col_count]  2.46 us
    ppermute x2, waiting for transfers between devices, passed_along(): return lax.ppermute(x, axis, pairs)  2.21 us
  transfers between devices with their start and end apart: 6, of which 4 were waited for; matrix products, arithmetic and copies ran while one was open for 0% of the time, Pallas kernels for 0%

profile of v1, /device:TPU:0, one launch (start us, length us, event | category | flops | bytes accessed | tf_op | source)
XLA Modules:
  0.0 95.1 jit_solution(59439621330333198)
XLA Ops:
  0.0 1.1 %convert_reduce_fusion = (f32[128]{0:T(128)S(1)}, f32[128]{0:T(128)S(1)}) fusion(bf16[2,2,256,128]{3,2,1,0:T(8,128)(2,1)} %param.8), kind=kLoop, calls=%fused_computation.36 | loop fusion | flops 524032 | bytes 263168 | tf_op jit(solution)/shard_map/reduce_sum | solution.py:36
  1.3 0.1 reduce_sum.73
  1.4 0.1 reduce_sum.75
  1.5 2.6 %all-reduce.5 = (f32[32]{0:T(128)S(1)}, f32[32]{0:T(128)S(1)}) all-reduce(f32[32]{0:T(128)S(1)} %reduce_sum.75, f32[32]{0:T(128)S(1)} %reduce_sum.73), channel_id=1, replica_groups=mesh['grp'=2,'tile'=8,'tm'=2] {'tm'}, use_global_device_ids=true, to_apply=%region_6.0 | all-reduce | flops 64 | bytes 512 | tf_op jit(solution)/shard_map/psum | solution.py:38
  4.1 23.0 %all-reduce.3 = (f32[32]{0:T(128)S(1)}, f32[32]{0:T(128)S(1)}) all-reduce(f32[32]{0:T(128)S(1)} %get-tuple-element.15, f32[32]{0:T(128)S(1)} %get-tuple-element.16), channel_id=1, replica_groups=mesh['grp'=2,'tile'=8,'tm'=2] {'tile'}, use_global_device_ids=true, to_apply=%region_7.0 | all-reduce | flops 64 | bytes 512 | tf_op jit(solution)/shard_map/psum | solution.py:38
  27.2 0.1 mul.59
  27.5 1.2 %fusion.116 = bf16[2,2,256,128]{3,2,1,0:T(8,128)(2,1)S(1)} fusion(bf16[2,2,256,128]{3,2,1,0:T(8,128)(2,1)} %param.8, f32[128]{0:T(128)} %param.12, f32[128]{0:T(128)} %param.11, f32[128]{0:T(128)S(1)} %mul.59, f32[128]{0:T(128)S(1)} %sub.26), kind=kLoop, calls=%fused_computation.151 | loop fusion | flops 1310720 | bytes 526336 | tf_op jit(solution)/shard_map/convert_element_type | solution.py:50
  28.7 1.4 %collective-permute-start = (bf16[2,2,256,128]{3,2,1,0:T(8,128)(2,1)S(1)}, bf16[2,2,256,128]{3,2,1,0:T(8,128)(2,1)S(1)}, u32[]{:S(2)}, u32[]{:S(2)}) collective-permute-start(bf16[2,2,256,128]{3,2,1,0:T(8,128)(2,1)S(1)} %fusion.116), channel_id=1, source_target_pairs={{0,1},{2,3},{4,5},{6,7},{8,9},{10,11},{12,13},{14,15},{16,17},{18,... | collective-permute-start | bytes 786440 | tf_op jit(solution)/shard_map/ppermute | solution.py:13
  30.1 1.1 %collective-permute-done = bf16[2,2,256,128]{3,2,1,0:T(8,128)(2,1)S(1)} collective-permute-done((bf16[2,2,256,128]{3,2,1,0:T(8,128)(2,1)S(1)}, bf16[2,2,256,128]{3,2,1,0:T(8,128)(2,1)S(1)}, u32[]{:S(2)}, u32[]{:S(2)}) %collective-permute-start) | collective-permute-done | bytes 262176 | tf_op jit(solution)/shard_map/ppermute | solution.py:13
  31.3 1.3 %collective-permute-start.1 = (bf16[4,1,256,128]{3,2,1,0:T(8,128)(2,1)S(1)}, bf16[4,1,256,128]{3,2,1,0:T(8,128)(2,1)S(1)}, u32[]{:S(2)}, u32[]{:S(2)}) collective-permute-start(bf16[4,1,256,128]{3,2,1,0:T(8,128)(2,1)S(1)} %get-tuple-element.89), channel_id=1, source_target_pairs={{0,2},{2,4},{4,6},{6,8},{8,10},{10,12},{12,14},{1,3},{3,5},{5,7},{... | collective-permute-start | bytes 786440 | tf_op jit(solution)/shard_map/ppermute | solution.py:24
  32.6 1.3 %collective-permute-start.2 = (bf16[4,1,256,128]{3,2,1,0:T(8,128)(2,1)S(1)}, bf16[4,1,256,128]{3,2,1,0:T(8,128)(2,1)S(1)}, u32[]{:S(2)}, u32[]{:S(2)}) collective-permute-start(bf16[4,1,256,128]{3,2,1,0:T(8,128)(2,1)S(1)} %get-tuple-element.90), channel_id=1, source_target_pairs={{2,0},{4,2},{6,4},{8,6},{10,8},{12,10},{14,12},{3,1},{5,3},{7,5},{... | collective-permute-start | bytes 786440 | tf_op jit(solution)/shard_map/ppermute | solution.py:26
  34.0 10.6 %collective-permute-done.1 = bf16[4,1,256,128]{3,2,1,0:T(8,128)(2,1)S(1)} collective-permute-done((bf16[4,1,256,128]{3,2,1,0:T(8,128)(2,1)S(1)}, bf16[4,1,256,128]{3,2,1,0:T(8,128)(2,1)S(1)}, u32[]{:S(2)}, u32[]{:S(2)}) %collective-permute-start.1) | collective-permute-done | bytes 262176 | tf_op jit(solution)/shard_map/ppermute | solution.py:24
  44.6 0.3 fusion.11
  44.9 1.0 %fusion.142 = (bf16[2,2,256,128]{3,2,1,0:T(8,128)(2,1)S(1)}, bf16[2,2,256,128]{3,2,1,0:T(8,128)(2,1)S(1)}, bf16[2,2,256,128]{3,2,1,0:T(8,128)(2,1)S(1)}, bf16[2,...) fusion(bf16[4,4,258,128]{3,2,1,0:T(8,128)(2,1)S(1)} %fusion.11), kind=kLoop, calls=%fused_computation.185 | loop fusion | bytes 9437184 | tf_op jit(solution)/shard_map/slice | solution.py:71
  45.9 0.1 pad_maximum_fusion.2
  46.0 0.3 fusion.147
  46.3 0.4 fusion.22
  46.7 0.4 convolution_add_fusion.15
  47.1 0.4 convolution_add_fusion.14
  47.4 0.4 convolution_add_fusion.13
  47.8 0.4 convolution_add_fusion.12
  48.2 0.4 convolution_add_fusion.11
  48.6 0.4 convolution_add_fusion.10
  48.9 0.4 convolution_add_fusion.9
  49.3 0.4 fusion.140
  49.8 0.1 reduce_sum.77
  50.1 0.1 reduce_sum.79
  50.2 2.5 %all-reduce.4 = (f32[32]{0:T(128)S(1)}, f32[32]{0:T(128)S(1)}) all-reduce(f32[32]{0:T(128)S(1)} %reduce_sum.79, f32[32]{0:T(128)S(1)} %reduce_sum.77), channel_id=1, replica_groups=mesh['grp'=2,'tile'=8,'tm'=2] {'tm'}, use_global_device_ids=true, to_apply=%region_14.15 | all-reduce | flops 64 | bytes 512 | tf_op jit(solution)/shard_map/psum | solution.py:38
  52.7 19.6 %all-reduce.2 = (f32[32]{0:T(128)S(1)}, f32[32]{0:T(128)S(1)}) all-reduce(f32[32]{0:T(128)S(1)} %get-tuple-element.13, f32[32]{0:T(128)S(1)} %get-tuple-element.14), channel_id=1, replica_groups=mesh['grp'=2,'tile'=8,'tm'=2] {'tile'}, use_global_device_ids=true, to_apply=%region_15.16 | all-reduce | flops 64 | bytes 512 | tf_op jit(solution)/shard_map/psum | solution.py:38
  72.3 0.1 mul.67
  72.7 0.2 multiply_convert_fusion
  72.9 1.4 %collective-permute-start.3 = (bf16[2,2,256,128]{3,2,1,0:T(8,128)(2,1)S(1)}, bf16[2,2,256,128]{3,2,1,0:T(8,128)(2,1)S(1)}, u32[]{:S(2)}, u32[]{:S(2)}) collective-permute-start(bf16[2,2,256,128]{3,2,1,0:T(8,128)(2,1)S(1)} %multiply_convert_fusion), channel_id=1, source_target_pairs={{0,1},{2,3},{4,5},{6,7},{8,9},{10,11},{12,13},{14,15},{16,17},{18,... | collective-permute-start | bytes 786440 | tf_op jit(solution)/shard_map/ppermute | solution.py:13
  74.3 1.1 %collective-permute-done.3 = bf16[2,2,256,128]{3,2,1,0:T(8,128)(2,1)S(1)} collective-permute-done((bf16[2,2,256,128]{3,2,1,0:T(8,128)(2,1)S(1)}, bf16[2,2,256,128]{3,2,1,0:T(8,128)(2,1)S(1)}, u32[]{:S(2)}, u32[]{:S(2)}) %collective-permute-start.3) | collective-permute-done | bytes 262176 | tf_op jit(solution)/shard_map/ppermute | solution.py:13
  75.5 1.5 %collective-permute-start.4 = (bf16[4,1,256,128]{3,2,1,0:T(8,128)(2,1)S(1)}, bf16[4,1,256,128]{3,2,1,0:T(8,128)(2,1)S(1)}, u32[]{:S(2)}, u32[]{:S(2)}) collective-permute-start(bf16[4,1,256,128]{3,2,1,0:T(8,128)(2,1)S(1)} %get-tuple-element.85), channel_id=1, source_target_pairs={{0,2},{2,4},{4,6},{6,8},{8,10},{10,12},{12,14},{1,3},{3,5},{5,7},{... | collective-permute-start | bytes 786440 | tf_op jit(solution)/shard_map/ppermute | solution.py:24
  77.0 1.3 %collective-permute-start.5 = (bf16[4,1,256,128]{3,2,1,0:T(8,128)(2,1)S(1)}, bf16[4,1,256,128]{3,2,1,0:T(8,128)(2,1)S(1)}, u32[]{:S(2)}, u32[]{:S(2)}) collective-permute-start(bf16[4,1,256,128]{3,2,1,0:T(8,128)(2,1)S(1)} %get-tuple-element.86), channel_id=1, source_target_pairs={{2,0},{4,2},{6,4},{8,6},{10,8},{12,10},{14,12},{3,1},{5,3},{7,5},{... | collective-permute-start | bytes 786440 | tf_op jit(solution)/shard_map/ppermute | solution.py:26
  78.4 10.4 %collective-permute-done.4 = bf16[4,1,256,128]{3,2,1,0:T(8,128)(2,1)S(1)} collective-permute-done((bf16[4,1,256,128]{3,2,1,0:T(8,128)(2,1)S(1)}, bf16[4,1,256,128]{3,2,1,0:T(8,128)(2,1)S(1)}, u32[]{:S(2)}, u32[]{:S(2)}) %collective-permute-start.4) | collective-permute-done | bytes 262176 | tf_op jit(solution)/shard_map/ppermute | solution.py:24
  89.0 0.3 select_maximum_fusion
  89.3 1.0 %fusion.141 = (bf16[2,2,256,128]{3,2,1,0:T(8,128)(2,1)S(1)}, bf16[2,2,256,128]{3,2,1,0:T(8,128)(2,1)S(1)}, bf16[2,2,256,128]{3,2,1,0:T(8,128)(2,1)S(1)}, bf16[2,...) fusion(bf16[4,4,258,128]{3,2,1,0:T(8,128)(2,1)S(1)} %select_max, ...), kind=kLoop, calls=%fused_computation.184 | loop fusion | bytes 9437184 | tf_op jit(solution)/shard_map/slice | solution.py:71
  90.4 0.4 fusion.65
  90.8 0.4 convolution_add_fusion.7
  91.2 0.4 convolution_add_fusion.6
  91.6 0.4 convolution_add_fusion.5
  91.9 0.4 convolution_add_fusion.4
  92.3 0.4 convolution_add_fusion.3
  92.7 0.4 convolution_add_fusion.2
  93.1 0.4 convolution_add_fusion.1
  93.5 0.6 copy-done
  94.0 1.1 %fusion.3 = bf16[2,2,256,128]{3,2,1,0:T(8,128)(2,1)} fusion(f32[2,2,256,128]{3,2,1,0:T(8,128)S(1)} %convolution_add_fusion.1, bf16[384,128,1,1]{1,0,3,2:T(8,128)(2,1)S(1)} %bitcast.109, bf16[2,2,256,128]{3,2,1,0:T(8,128)(2,1)S(1)} %copy-done, bf16[2,2,256,128]{3,2,1,0:T(8,128)(2,1)S(1)} %get-tuple-element.34, ...), kind=kOutput, calls=%fused_computation.21 | convolution fusion | flops 103677952 | bytes 1933824 | tf_op jit(solution)/shard_map/dot_general | solution.py:74
  (36 shorter events, 1.6 us)
Async XLA Ops:
  28.6 5.3 %copy-start.1 = (bf16[3,3,3,128,128]{4,3,2,1,0:T(8,128)(2,1)S(1)}, bf16[3,3,3,128,128]{4,3,2,1,0:T(8,128)(2,1)}, u32[]{:S(2)}) copy-start(bf16[3,3,3,128,128]{4,3,2,1,0:T(8,128)(2,1)} %param.9) | copy-start | bytes 2654212
  28.7 2.6 %collective-permute-start = (bf16[2,2,256,128]{3,2,1,0:T(8,128)(2,1)S(1)}, bf16[2,2,256,128]{3,2,1,0:T(8,128)(2,1)S(1)}, u32[]{:S(2)}, u32[]{:S(2)}) collective-permute-start(bf16[2,2,256,128]{3,2,1,0:T(8,128)(2,1)S(1)} %fusion.116), channel_id=1, source_target_pairs={{0,1},{2,3},{4,5},{6,7},{8,9},{10,11},{12,13},{14,15},{16,17},{18,... | collective-permute-start | bytes 786440 | tf_op jit(solution)/shard_map/ppermute | solution.py:13
  31.3 13.3 %collective-permute-start.1 = (bf16[4,1,256,128]{3,2,1,0:T(8,128)(2,1)S(1)}, bf16[4,1,256,128]{3,2,1,0:T(8,128)(2,1)S(1)}, u32[]{:S(2)}, u32[]{:S(2)}) collective-permute-start(bf16[4,1,256,128]{3,2,1,0:T(8,128)(2,1)S(1)} %get-tuple-element.89), channel_id=1, source_target_pairs={{0,2},{2,4},{4,6},{6,8},{8,10},{10,12},{12,14},{1,3},{3,5},{5,7},{... | collective-permute-start | bytes 786440 | tf_op jit(solution)/shard_map/ppermute | solution.py:24
  32.6 12.0 %collective-permute-start.2 = (bf16[4,1,256,128]{3,2,1,0:T(8,128)(2,1)S(1)}, bf16[4,1,256,128]{3,2,1,0:T(8,128)(2,1)S(1)}, u32[]{:S(2)}, u32[]{:S(2)}) collective-permute-start(bf16[4,1,256,128]{3,2,1,0:T(8,128)(2,1)S(1)} %get-tuple-element.90), channel_id=1, source_target_pairs={{2,0},{4,2},{6,4},{8,6},{10,8},{12,10},{14,12},{3,1},{5,3},{7,5},{... | collective-permute-start | bytes 786440 | tf_op jit(solution)/shard_map/ppermute | solution.py:26
  49.3 23.3 %copy-start.3 = (f32[128]{0:T(128)S(1)}, f32[128]{0:T(128)}, u32[]{:S(2)}) copy-start(f32[128]{0:T(128)} %param.14) | copy-start | bytes 1540
  49.3 23.3 %copy-start.4 = (f32[128]{0:T(128)S(1)}, f32[128]{0:T(128)}, u32[]{:S(2)}) copy-start(f32[128]{0:T(128)} %param.13) | copy-start | bytes 1540
  72.8 5.5 %copy-start.2 = (bf16[3,3,3,128,128]{4,3,2,1,0:T(8,128)(2,1)S(1)}, bf16[3,3,3,128,128]{4,3,2,1,0:T(8,128)(2,1)}, u32[]{:S(2)}) copy-start(bf16[3,3,3,128,128]{4,3,2,1,0:T(8,128)(2,1)} %param.10) | copy-start | bytes 2654212
  72.9 2.6 %collective-permute-start.3 = (bf16[2,2,256,128]{3,2,1,0:T(8,128)(2,1)S(1)}, bf16[2,2,256,128]{3,2,1,0:T(8,128)(2,1)S(1)}, u32[]{:S(2)}, u32[]{:S(2)}) collective-permute-start(bf16[2,2,256,128]{3,2,1,0:T(8,128)(2,1)S(1)} %multiply_convert_fusion), channel_id=1, source_target_pairs={{0,1},{2,3},{4,5},{6,7},{8,9},{10,11},{12,13},{14,15},{16,17},{18,... | collective-permute-start | bytes 786440 | tf_op jit(solution)/shard_map/ppermute | solution.py:13
  75.5 13.3 %collective-permute-start.4 = (bf16[4,1,256,128]{3,2,1,0:T(8,128)(2,1)S(1)}, bf16[4,1,256,128]{3,2,1,0:T(8,128)(2,1)S(1)}, u32[]{:S(2)}, u32[]{:S(2)}) collective-permute-start(bf16[4,1,256,128]{3,2,1,0:T(8,128)(2,1)S(1)} %get-tuple-element.85), channel_id=1, source_target_pairs={{0,2},{2,4},{4,6},{6,8},{8,10},{10,12},{12,14},{1,3},{3,5},{5,7},{... | collective-permute-start | bytes 786440 | tf_op jit(solution)/shard_map/ppermute | solution.py:24
  77.0 11.8 %collective-permute-start.5 = (bf16[4,1,256,128]{3,2,1,0:T(8,128)(2,1)S(1)}, bf16[4,1,256,128]{3,2,1,0:T(8,128)(2,1)S(1)}, u32[]{:S(2)}, u32[]{:S(2)}) collective-permute-start(bf16[4,1,256,128]{3,2,1,0:T(8,128)(2,1)S(1)} %get-tuple-element.86), channel_id=1, source_target_pairs={{2,0},{4,2},{6,4},{8,6},{10,8},{12,10},{14,12},{3,1},{5,3},{7,5},{... | collective-permute-start | bytes 786440 | tf_op jit(solution)/shard_map/ppermute | solution.py:26
  93.1 1.0 %copy-start = (bf16[2,2,256,128]{3,2,1,0:T(8,128)(2,1)S(1)}, bf16[2,2,256,128]{3,2,1,0:T(8,128)(2,1)}, u32[]{:S(2)}) copy-start(bf16[2,2,256,128]{3,2,1,0:T(8,128)(2,1)} %param.8) | copy-start | bytes 786436
  93.1 0.9 copy-start.5
